TPU v7x, 32 devices: a whole 2x2x4 slice. The times are simulated.
32 devices in a mesh: sec: 2 (over core), req: 4 (over z), kv: 4 (over y, x).
Axes of the slice: x: 2, y: 2, z: 4, core: 2. Of those that a mesh axis runs over, the one named last changes fastest.
Arguments:
- queries: bfloat16 [512, 4096], P('req', ('kv', 'sec')), may hold values from -21 to 21
- key_cache: bfloat16 [512, 4, 32, 128], P('req', 'kv'), may hold values from -21 to 21
- value_cache: bfloat16 [512, 4, 32, 128], P('req', 'kv'), may hold values from -18 to 18
- new_keys: bfloat16 [512, 4, 128], P('req', 'kv'), may hold values from -5 to 5
- new_values: bfloat16 [512, 4, 128], P('req', 'kv'), may hold values from -18 to 18
- lengths: int32 [512], P('req'), may hold values from 2 to 32
- out_proj: bfloat16 [4096, 4096], P(('kv', 'sec')), may hold values from -0.09375 to 0.09375
- residual: bfloat16 [512, 4096], P(('req', 'sec', 'kv')), may hold values from -36 to 36
- norm_gain: float32 [4096], replicated, may hold values from 0.1 to 1.9
- expert_ids: int32 [512, 8], P(('req', 'sec', 'kv')), may hold values from 0 to 31, as said below
- expert_slots: int32 [512, 8], P(('req', 'sec', 'kv')), may hold values from 0 to 4, as said below
- gate_probs: float32 [512, 8], P(('req', 'sec', 'kv')), may hold values from 0.1 to 0.4
- w_gate: bfloat16 [32, 4096, 768], P(('sec', 'req', 'kv')), may hold values from -0.09375 to 0.09375
- w_up: bfloat16 [32, 4096, 768], P(('sec', 'req', 'kv')), may hold values from -0.09375 to 0.09375
- w_down: bfloat16 [32, 768, 4096], P(('sec', 'req', 'kv')), may hold values from -0.21875 to 0.21875
Outputs:
- stream: bfloat16 [512, 4096], P(('req', 'sec', 'kv'))
- moe_out: bfloat16 [512, 4096], P(('req', 'sec', 'kv'))
Inputs may be any that keep to these rules, and one draw needn't show every extreme that they name: `expert_ids`: each row names 8 different experts. In each block of 16 consecutive rows (the rows of one device) every expert is named at least 3 and at most 5 times, and one expert, the same for all blocks, exactly 5 times. `expert_slots`: within a block the entries naming one expert hold different slots, numbered from 0 in row order.
All inputs are finite; a program needn't handle non-finite values.
Results may differ from a plain program's by a relative error of at most 0.029.
Values may be sent and summed in bfloat16 or wider, within the bound.
A program may use at most 128 MiB of HBM per device.

v0:
```python
import jax
import jax.numpy as jnp
from jax import lax
from jax.sharding import PartitionSpec as P


def on_device(
    queries,
    key_cache,
    value_cache,
    new_keys,
    new_values,
    lengths,
    out_proj,
    residual,
    norm_gain,
    expert_ids,
    expert_slots,
    gate_probs,
    w_gate,
    w_up,
    w_down,
):
    row_count, head_width = queries.shape
    head_size = key_cache.shape[3]
    positions = key_cache.shape[2]
    heads_here = head_width // head_size
    width = out_proj.shape[1]
    score_scale = 1.0 / head_size**0.5
    query_heads = queries.reshape(row_count, heads_here, head_size)
    score = (
        jnp.einsum("thd,tpd->thp", query_heads, key_cache[:, 0], preferred_element_type=jnp.float32)
        * score_scale
    )
    own_score = (
        jnp.einsum("thd,td->th", query_heads, new_keys[:, 0], preferred_element_type=jnp.float32)
        * score_scale
    )
    valid = jnp.arange(positions, dtype=jnp.int32)[None, :] < lengths[:, None]
    score = jnp.where(valid[:, None, :], score, -jnp.inf)
    highest = jnp.maximum(jnp.max(score, axis=-1), own_score)
    raised = jnp.exp(score - highest[..., None])
    own_raised = jnp.exp(own_score - highest)
    denominator = jnp.sum(raised, axis=-1) + own_raised
    weight = (raised / denominator[..., None]).astype(jnp.bfloat16)
    own_weight = (own_raised / denominator).astype(jnp.bfloat16)
    attn = jnp.einsum("thp,tpd->thd", weight, value_cache[:, 0], preferred_element_type=jnp.float32)
    attn = (
        attn
        + own_weight.astype(jnp.float32)[..., None]
        * new_values[:, 0].astype(jnp.float32)[:, None, :]
    )
    attn = attn.astype(jnp.bfloat16).reshape(row_count, head_width)
    sec_count = lax.axis_size("sec")
    group_count = lax.axis_size("kv")
    row_share = row_count // (sec_count * group_count)
    proj = lax.psum_scatter(
        jnp.dot(attn, out_proj, preferred_element_type=jnp.float32).astype(jnp.bfloat16),
        ("sec", "kv"),
        scatter_dimension=0,
        tiled=True,
    ).astype(jnp.float32)
    stream = (residual.astype(jnp.float32) + proj).astype(jnp.bfloat16)
    widened = lax.optimization_barrier(stream).astype(jnp.float32)
    mean_square = jnp.mean(widened * widened, axis=-1, keepdims=True)
    normed = (widened * lax.rsqrt(mean_square + 1e-06) * norm_gain).astype(jnp.bfloat16)
    expert_count = sec_count * lax.axis_size("req") * group_count
    top_count = expert_ids.shape[1]
    capacity = top_count * row_share // expert_count + 1
    slot_index = (expert_ids * capacity + expert_slots).reshape(-1)
    repeated = jnp.broadcast_to(normed[:, None, :], (row_share, top_count, width)).reshape(
        row_share * top_count, width
    )
    outgoing = (
        jnp.zeros((expert_count * capacity, width), jnp.bfloat16).at[slot_index].set(repeated)
    )
    arrived = lax.all_to_all(
        outgoing.reshape(expert_count, capacity, width),
        ("sec", "req", "kv"),
        split_axis=0,
        concat_axis=0,
        tiled=True,
    )
    flat_rows = arrived.reshape(-1, width)
    gate_out = jnp.dot(flat_rows, w_gate[0], preferred_element_type=jnp.float32)
    up_out = jnp.dot(flat_rows, w_up[0], preferred_element_type=jnp.float32)
    hidden = (jax.nn.silu(gate_out) * up_out).astype(jnp.bfloat16)
    finished = jnp.dot(hidden, w_down[0], preferred_element_type=jnp.float32).astype(jnp.bfloat16)
    returned = lax.all_to_all(
        finished.reshape(arrived.shape),
        ("sec", "req", "kv"),
        split_axis=0,
        concat_axis=0,
        tiled=True,
    )
    picked = returned.reshape(expert_count * capacity, width)[slot_index].reshape(
        row_share, top_count, width
    )
    moe_out = jnp.sum(picked.astype(jnp.float32) * gate_probs[..., None], axis=1).astype(
        jnp.bfloat16
    )
    return (stream, moe_out)


def solution(mesh):
    return jax.shard_map(
        on_device,
        mesh=mesh,
        in_specs=(
            P("req", ("kv", "sec")),
            P("req", "kv", None, None),
            P("req", "kv", None, None),
            P("req", "kv", None),
            P("req", "kv", None),
            P("req"),
            P(("kv", "sec"), None),
            P(("req", "sec", "kv"), None),
            P(),
            P(("req", "sec", "kv"), None),
            P(("req", "sec", "kv"), None),
            P(("req", "sec", "kv"), None),
            P(("sec", "req", "kv"), None, None),
            P(("sec", "req", "kv"), None, None),
            P(("sec", "req", "kv"), None, None),
        ),
        out_specs=(P(("req", "sec", "kv"), None), P(("req", "sec", "kv"), None)),
        check_vma=False,
    )
```

profile of v0, /device:TPU:0, one launch (start us, length us, event | category | flops | bytes accessed | tf_op | source)
XLA Modules:
  0.0 200.2 jit_solution(5099958744358083993)
XLA Ops:
  7.2 1.0 reshape.90
  8.3 0.7 iota_compare_fusion
  9.0 2.0 fusion.47
  11.0 1.1 fusion.40
  12.2 0.1 copy.27
  12.3 0.4 fusion.35
  12.8 0.1 copy.29
  13.0 0.5 fusion.17
  13.6 3.9 %convolution_convert_fusion = bf16[128,4096]{1,0:T(8,128)(2,1)} fusion(bf16[512,4096]{1,0:T(8,128)(2,1)} %param.21, bf16[16,8,4,128]{3,2,1,0:T(4,128)(2,1)S(1)} %bitcast.63), kind=kOutput, calls=%fused_computation.9 | convolution fusion | flops 537395200 | bytes 5373952 | tf_op jit(solution)/shard_map/dot_general | solution.py:58
  17.7 38.7 %reduce-scatter.2.cloned.1.call-done = bf16[16,4096]{1,0:T(8,128)(2,1)} async-done(((bf16[128,4096]{1,0:T(8,128)(2,1)}), bf16[16,4096]{1,0:T(8,128)(2,1)}) %reduce-scatter.2.cloned.1.call-update) | async-done | bytes 131088 | tf_op jit(solution)/shard_map/reduce_scatter | solution.py:57
  56.4 0.9 add_convert_fusion
  57.4 0.1 fusion.31
  57.6 3.2 %scatter_custom_fusion = bf16[160,4096]{1,0:T(8,128)(2,1)} fusion(s32[128]{0:T(128)S(1)} %fusion.44, bf16[]{:T(256)} %constant.4.clone.1, bf16[16,4096]{1,0:T(8,128)(2,1)S(1)} %fusion.33), kind=kCustom, calls=%fused_computation.18 | custom fusion | bytes 1441794 | tf_op jit(solution)/shard_map/scatter | solution.py:75
  60.8 1.6 reshape.94
  62.5 55.0 %all_to_all.10 = bf16[32,5,4096]{2,1,0:T(8,128)(2,1)} all-to-all(bf16[32,5,4096]{2,1,0:T(8,128)(2,1)S(1)} %reshape.94), channel_id=1, replica_groups=mesh['sec'=2,'req'=4,'kv'=4] {'sec','req','kv'}, dimensions={0} | all-to-all | bytes 2621440 | tf_op jit(solution)/shard_map/all_to_all | solution.py:77
  117.5 1.8 reshape.95
  119.3 4.0 %fusion.4 = f32[160,768]{1,0:T(8,128)S(1)} fusion(bf16[160,4096]{1,0:T(8,128)(2,1)S(1)} %reshape.95, bf16[1,4096,768]{2,1,0:T(8,128)(2,1)} %param.27), kind=kOutput, calls=%fused_computation.6 | convolution fusion | flops 1006632960 | bytes 8093696 | tf_op jit(solution)/shard_map/dot_general | solution.py:85
  123.3 8.6 %fusion.6 = bf16[160,4096]{1,0:T(8,128)(2,1)} fusion(bf16[1,768,4096]{2,1,0:T(8,128)(2,1)} %param.29, bf16[160,4096]{1,0:T(8,128)(2,1)S(1)} %reshape.95, bf16[1,4096,768]{2,1,0:T(8,128)(2,1)} %param.28, f32[160,768]{1,0:T(8,128)S(1)} %fusion.4), kind=kOutput, calls=%fused_computation.8 | convolution fusion | flops 2014658560 | bytes 15695872 | tf_op jit(solution)/shard_map/dot_general | solution.py:88
  131.9 2.7 %reshape.96 = bf16[32,5,4096]{2,1,0:T(8,128)(2,1)} reshape(bf16[160,4096]{1,0:T(8,128)(2,1)} %fusion.6) | data formatting | bytes 2621440 | tf_op jit(solution)/shard_map/reshape | solution.py:90
  134.7 3.6 %all-to-all-start.1 = ((bf16[32,5,4096]{2,1,0:T(8,128)(2,1)}), bf16[32,5,4096]{2,1,0:T(8,128)(2,1)}, u32[]{:S(2)}, u32[]{:S(2)}) async-start(bf16[32,5,4096]{2,1,0:T(8,128)(2,1)} %reshape.96), calls=%async_computation.2 | async-start | bytes 4194304 | tf_op jit(solution)/shard_map/all_to_all | solution.py:89
  138.4 50.5 %all-to-all-done.1 = bf16[32,5,4096]{2,1,0:T(8,128)(2,1)} async-done(((bf16[32,5,4096]{2,1,0:T(8,128)(2,1)}), bf16[32,5,4096]{2,1,0:T(8,128)(2,1)}, u32[]{:S(2)}, u32[]{:S(2)}) %all-to-all-start.1) | async-done | bytes 1310752 | tf_op jit(solution)/shard_map/all_to_all | solution.py:89
  188.9 1.8 reshape.97
  190.7 1.2 gather_fusion
  191.9 1.4 fusion.9
  (33 shorter events, 0.8 us)
Async XLA Ops:
  7.2 5.9 %copy-start = (bf16[128,1,32,128]{3,2,1,0:T(8,128)(2,1)S(1)}, bf16[128,1,32,128]{3,2,1,0:T(8,128)(2,1)}, u32[]{:S(2)}) copy-start(bf16[128,1,32,128]{3,2,1,0:T(8,128)(2,1)} %param.17) | copy-start | bytes 3145732
  7.2 5.8 %copy-start.3 = (bf16[128,1,128]{2,0,1:T(8,128)(2,1)S(1)}, bf16[128,1,128]{2,0,1:T(8,128)(2,1)}, u32[]{:S(2)}) copy-start(bf16[128,1,128]{2,0,1:T(8,128)(2,1)} %param.19) | copy-start | bytes 98308
  7.2 49.2 %reduce-scatter.2.cloned.1.call-start = ((), (), s32[]{:S(2)}) async-start(), calls=%async_computation.3 | async-start | bytes 1179648 | tf_op jit(solution)/shard_map/reduce_scatter | solution.py:57
  13.5 4.0 %copy-start.5 = (s32[16,8]{0,1:T(8,128)S(1)}, s32[16,8]{0,1:T(8,128)}, u32[]{:S(2)}) copy-start(s32[16,8]{0,1:T(8,128)} %param.25) | copy-start | bytes 1540
  13.5 4.0 %copy-start.6 = (s32[16,8]{0,1:T(8,128)S(1)}, s32[16,8]{0,1:T(8,128)}, u32[]{:S(2)}) copy-start(s32[16,8]{0,1:T(8,128)} %param.24) | copy-start | bytes 1540
  13.6 42.9 %copy-start.2 = (bf16[16,4096]{1,0:T(8,128)(2,1)S(1)}, bf16[16,4096]{1,0:T(8,128)(2,1)}, u32[]{:S(2)}) copy-start(bf16[16,4096]{1,0:T(8,128)(2,1)} %param.22) | copy-start | bytes 393220
  13.6 44.0 %copy-start.4 = (f32[4096]{0:T(1024)S(1)}, f32[4096]{0:T(1024)}, u32[]{:S(2)}) copy-start(f32[4096]{0:T(1024)} %param.23) | copy-start | bytes 49156
  57.4 5.1 %copy-start.1 = (bf16[16,4096]{1,0:T(8,128)(2,1)}, bf16[16,4096]{1,0:T(8,128)(2,1)S(1)}, u32[]{:S(2)}) copy-start(bf16[16,4096]{1,0:T(8,128)(2,1)S(1)} %add_convert_fusion) | copy-start | bytes 393220
  134.7 3.6 %copy-start.7 = (f32[16,8]{0,1:T(8,128)S(1)}, f32[16,8]{0,1:T(8,128)}, u32[]{:S(2)}) copy-start(f32[16,8]{0,1:T(8,128)} %param.26) | copy-start | bytes 1540
  134.7 54.2 %all-to-all-start.1 = ((bf16[32,5,4096]{2,1,0:T(8,128)(2,1)}), bf16[32,5,4096]{2,1,0:T(8,128)(2,1)}, u32[]{:S(2)}, u32[]{:S(2)}) async-start(bf16[32,5,4096]{2,1,0:T(8,128)(2,1)} %reshape.96), calls=%async_computation.2 | async-start | bytes 4194304 | tf_op jit(solution)/shard_map/all_to_all | solution.py:89
Sparse Core Ops, SparseCore 0:
  17.7 38.7 reduce-scatter.1
where the time goes:
time: 201 us; the launch traced here: 200 us
  waiting for transfers between devices  89.2 us (44%)
  blocking collectives  55 us (27%)
  matrix products  20 us (10%)
  between operations  14.3 us (7%)
  local copies, waits for them, and re-layouts  14.2 us (7%)
  other arithmetic  3.82 us (2%)
  starting transfers between devices  3.65 us (2%)
    all_to_all x1, blocking collectives, on_device(): lax.all_to_all(outgoing.reshape(expert_count, capacity, width), ('sec', '...  55 us
    all_to_all x1, waiting for transfers between devices, on_device(): lax.all_to_all(finished.reshape(arrived.shape), ('sec', 'req', 'kv'), spl...  50.5 us
    reduce_scatter x1, waiting for transfers between devices, on_device(): lax.psum_scatter(jnp.dot(attn, out_proj, preferred_element_type=jnp.float...  38.7 us
    dot_general x1, matrix products, on_device(): jnp.dot(hidden, w_down[0], preferred_element_type=jnp.float32)  8.63 us
  transfers between devices with their start and end apart: 2, of which 2 were waited for; matrix products, arithmetic and copies ran while one was open for 0% of the time, Pallas kernels for 0%

commit v1 on v0

v1 whole, which is shorter than its diff:
```python
import functools

import jax
import jax.numpy as jnp
import numpy as np
from jax import lax
from jax.experimental import pallas as pl
from jax.experimental.pallas import tpu as pltpu
from jax.sharding import PartitionSpec as P

MESH = pl.DeviceIdType.MESH
CHUNKS = 4
BF16 = jnp.bfloat16
F32 = jnp.float32


def dot(a, b):
    return jnp.dot(a, b, preferred_element_type=F32)


def layout(blocks, capacity):
    slots = blocks * capacity
    left = slots - 16
    if left in (1, 2, 4, 8):
        return 16, left
    return -(-slots // 16) * 16, 0


def layer_kernel(
    dims,
    attn_ref,
    out_proj_hbm,
    residual_ref,
    gain_ref,
    table_ref,
    col_ref,
    col_left_ref,
    row_ref,
    row_left_ref,
    unpack_ref,
    pack_ref,
    gate_hbm,
    up_hbm,
    down_hbm,
    stream_ref,
    moe_ref,
    out_proj,
    w_gate,
    w_up,
    w_down,
    sib_out,
    sib_in,
    part_out,
    part_in,
    tables,
    pick,
    pick_left,
    spread,
    spread_left,
    tokens,
    disp_out,
    disp_in,
    rows_in,
    gate_acc,
    up_acc,
    ret_out,
    ret_in,
    sum_out,
    sum_in,
    weight_sem,
    sib_sem,
    part_sem,
    table_sem,
    token_sem,
    disp_sem,
    ret_sem,
    sum_sem,
):
    R, K, full, left = dims["R"], dims["K"], dims["full"], dims["left"]
    top = dims["top"]
    M = 2 * K
    nch = CHUNKS
    width = stream_ref.shape[1]
    cw = width // nch
    parts = 16 // left if left else 0
    lw = cw // parts if left else 0
    s = lax.axis_index("sec")
    r = lax.axis_index("req")
    k = lax.axis_index("kv")
    m = s * K + k

    def cols(j):
        return pl.ds(pl.multiple_of(j * cw, cw), cw)

    def weight_copy(which, j):
        src, dst = [
            (out_proj_hbm.at[:, cols(j)], out_proj),
            (gate_hbm.at[0, cols(j)], w_gate),
            (up_hbm.at[0, cols(j)], w_up),
            (down_hbm.at[0, :, cols(j)], w_down),
        ][which]
        return pltpu.make_async_copy(src, dst.at[j], weight_sem.at[which, j])

    for which in range(4):
        for j in range(nch):
            weight_copy(which, j).start()

    def line(i):
        return lax.rem(r + i, R)

    def plane(i):
        return lax.rem(m + i, M)

    def remote(src, dst, sems, at, device):
        return pltpu.make_async_remote_copy(
            src_ref=src,
            dst_ref=dst,
            send_sem=sems.at[(0, *at)],
            recv_sem=sems.at[(1, *at)],
            device_id=device,
            device_id_type=MESH,
        )

    barrier = pltpu.get_barrier_semaphore()
    for i in range(1, M):
        p = plane(i)
        pl.semaphore_signal(
            barrier, inc=1, device_id=(p // K, r, lax.rem(p, K)), device_id_type=MESH
        )
    for i in range(1, R):
        pl.semaphore_signal(barrier, inc=1, device_id=(s, line(i), k), device_id_type=MESH)
    pl.semaphore_wait(barrier, M + R - 2)

    def table_copy(i, me):
        return remote(table_ref, tables.at[me], table_sem, (i - 1,), (s, line(i), k))

    def sib_copy(j):
        return remote(sib_out.at[j], sib_in.at[j], sib_sem, (j,), (1 - s, r, k))

    def part_copy(j, i):
        to = lax.rem(k + i, K)
        return remote(
            part_out.at[j, to], part_in.at[j, i - 1], part_sem, (j, i - 1), (s, r, to)
        )

    def token_copy(j, i, me):
        return remote(tokens.at[j, me], tokens.at[j, me], token_sem, (j, i - 1), (s, line(i), k))

    def plane_copy(out, into, sems, j, i, me):
        p = plane(i)
        return remote(out.at[j, p], into.at[j, me], sems, (j, i - 1), (p // K, r, lax.rem(p, K)))

    def sum_copy(j, i):
        to = line(i)
        return remote(sum_out.at[j, to], sum_in.at[j, i - 1], sum_sem, (j, i - 1), (s, to, k))

    def before(i):
        return lax.rem(r - i + R, R)

    def plane_before(i):
        return lax.rem(m - i + M, M)

    for i in range(1, R):
        table_copy(i, r).start()
    tables[r] = table_ref[...]

    @pl.loop(0, nch)
    def _(j):
        weight_copy(0, j).wait()
        sib_out[j] = dot(attn_ref[1 - s], out_proj[j]).astype(BF16)
        sib_copy(j).start()

    @pl.loop(0, nch)
    def _(j):
        own = dot(attn_ref[s], out_proj[j])
        sib_copy(j).wait_recv()
        part_out[j] = (own + sib_in[j].astype(F32)).astype(BF16).reshape(K, 16, cw)
        for i in range(1, K):
            part_copy(j, i).start()

    for i in range(1, R):
        table_copy(i, before(i)).wait_recv()
    codes = tables[0, 0:top, :]
    for q in range(1, R):
        codes = jnp.maximum(codes, tables[q, 0:top, :])
    codes = codes[:, : R * 16]

    def one_hot(targets):
        total = jnp.zeros((targets.shape[0], R * 16), F32)
        for n in range(top):
            total = total + jnp.where(codes[n : n + 1, :] == targets, 1.0, 0.0)
        return total.astype(BF16)

    def weighted(q, targets):
        total = jnp.zeros((16, targets.shape[1]), F32)
        entry = tables[q, top : top + 16, :]
        for n in range(top):
            total = total + jnp.where(
                entry[:, n : n + 1] == targets, entry[:, top + n : top + n + 1], 0.0
            )
        return total.astype(BF16)

    pick[...] = one_hot(col_ref[...])
    for q in range(parts):
        pick_left[q] = one_hot(col_left_ref[q])
    for q in range(R):
        spread[q * 16 : (q + 1) * 16, :] = weighted(q, row_ref[...])
        for n in range(parts):
            spread_left[n, q * 16 : (q + 1) * 16, :] = weighted(q, row_left_ref[n])

    def add_parts(j, squares):
        total = part_out[j, k].astype(F32)
        for i in range(1, K):
            part_copy(j, i).wait_recv()
            total = total + part_in[j, i - 1].astype(F32)
        value = (residual_ref[:, cols(j)].astype(F32) + total).astype(BF16)
        stream_ref[:, cols(j)] = value
        value = value.astype(F32)
        return squares + jnp.sum(value * value, axis=1, keepdims=True)

    squares = lax.fori_loop(0, nch, add_parts, jnp.zeros((16, 1), F32))
    scale = lax.rsqrt(squares * (1.0 / width) + 1e-06)

    @pl.loop(0, nch)
    def _(j):
        value = stream_ref[:, cols(j)].astype(F32)
        tokens[j, r] = (value * scale * gain_ref[:, cols(j)]).astype(BF16)
        for i in range(1, R):
            token_copy(j, i, r).start()

    @pl.loop(0, nch)
    def _(j):
        for i in range(1, R):
            token_copy(j, i, before(i)).wait_recv()
        held = tokens[j].reshape(R * 16, cw)
        disp_out[j, :, :, 0:cw] = dot(pick[...], held).astype(BF16).reshape(M, full, cw)
        if left:
            extra = dot(pick_left[0], held[:, 0:lw])
            for q in range(1, parts):
                extra = extra + dot(pick_left[q], held[:, q * lw : (q + 1) * lw])
            disp_out[j, :, :, cw : cw + lw] = extra.astype(BF16).reshape(M, 16, lw)
        for i in range(1, M):
            plane_copy(disp_out, disp_in, disp_sem, j, i, m).start()
        disp_in[j, m] = disp_out[j, m]

    gate_acc[...] = jnp.zeros_like(gate_acc)
    up_acc[...] = jnp.zeros_like(up_acc)

    @pl.loop(0, nch)
    def _(j):
        weight_copy(1, j).wait()
        weight_copy(2, j).wait()
        for i in range(1, M):
            plane_copy(disp_out, disp_in, disp_sem, j, i, plane_before(i)).wait_recv()
        rows_in[0 : M * full, :] = disp_in[j, :, :, 0:cw].reshape(M * full, cw)
        if left:
            extra = disp_in[j, :, :, cw : cw + lw].reshape(M * 16, lw)
            for q in range(parts):
                rows_in[M * full :, q * lw : (q + 1) * lw] = dot(unpack_ref[q], extra).astype(BF16)
        gate_acc[...] += dot(rows_in[...], w_gate[j])
        up_acc[...] += dot(rows_in[...], w_up[j])

    gate_out = gate_acc[...]
    hidden = (gate_out / (1.0 + jnp.exp(-gate_out)) * up_acc[...]).astype(BF16)

    @pl.loop(0, nch)
    def _(j):
        weight_copy(3, j).wait()
        finished = dot(hidden, w_down[j]).astype(BF16)
        ret_out[j, :, :, 0:cw] = finished[0 : M * full].reshape(M, full, cw)
        if left:
            rest = finished[M * full :]
            extra = dot(pack_ref[0], rest[:, 0:lw])
            for q in range(1, parts):
                extra = extra + dot(pack_ref[q], rest[:, q * lw : (q + 1) * lw])
            ret_out[j, :, :, cw : cw + lw] = extra.astype(BF16).reshape(M, 16, lw)
        for i in range(1, M):
            plane_copy(ret_out, ret_in, ret_sem, j, i, m).start()
        ret_in[j, m] = ret_out[j, m]

    @pl.loop(0, nch)
    def _(j):
        for i in range(1, M):
            plane_copy(ret_out, ret_in, ret_sem, j, i, plane_before(i)).wait_recv()
        total = dot(spread[...], ret_in[j, :, :, 0:cw].reshape(M * full, cw))
        if left:
            extra = ret_in[j, :, :, cw : cw + lw].reshape(M * 16, lw)
            total = total + jnp.concatenate(
                [dot(spread_left[q], extra) for q in range(parts)], axis=1
            )
        sum_out[j] = total.astype(BF16).reshape(R, 16, cw)
        for i in range(1, R):
            sum_copy(j, i).start()

    @pl.loop(0, nch)
    def _(j):
        total = sum_out[j, r].astype(F32)
        for i in range(1, R):
            sum_copy(j, i).wait_recv()
            total = total + sum_in[j, i - 1].astype(F32)
        moe_ref[:, cols(j)] = total.astype(BF16)

    for i in range(1, R):
        table_copy(i, r).wait_send()

    @pl.loop(0, nch)
    def _(j):
        sib_copy(j).wait_send()
        for i in range(1, K):
            part_copy(j, i).wait_send()
        for i in range(1, R):
            token_copy(j, i, r).wait_send()
            sum_copy(j, i).wait_send()
        for i in range(1, M):
            plane_copy(disp_out, disp_in, disp_sem, j, i, m).wait_send()
            plane_copy(ret_out, ret_in, ret_sem, j, i, m).wait_send()


def attention(queries, key_cache, value_cache, new_keys, new_values, lengths):
    row_count, head_width = queries.shape
    head_size = key_cache.shape[3]
    positions = key_cache.shape[2]
    heads_here = head_width // head_size
    score_scale = 1.0 / head_size**0.5
    query_heads = queries.reshape(row_count, heads_here, head_size)
    score = (
        jnp.einsum("thd,tpd->thp", query_heads, key_cache[:, 0], preferred_element_type=F32)
        * score_scale
    )
    own_score = (
        jnp.einsum("thd,td->th", query_heads, new_keys[:, 0], preferred_element_type=F32)
        * score_scale
    )
    valid = jnp.arange(positions, dtype=jnp.int32)[None, :] < lengths[:, None]
    score = jnp.where(valid[:, None, :], score, -jnp.inf)
    highest = jnp.maximum(jnp.max(score, axis=-1), own_score)
    raised = jnp.exp(score - highest[..., None])
    own_raised = jnp.exp(own_score - highest)
    denominator = jnp.sum(raised, axis=-1) + own_raised
    weight = (raised / denominator[..., None]).astype(BF16)
    own_weight = (own_raised / denominator).astype(BF16)
    attn = jnp.einsum("thp,tpd->thd", weight, value_cache[:, 0], preferred_element_type=F32)
    attn = attn + own_weight.astype(F32)[..., None] * new_values[:, 0].astype(F32)[:, None, :]
    return attn.astype(BF16).reshape(row_count, head_width)


def on_device(
    queries,
    key_cache,
    value_cache,
    new_keys,
    new_values,
    lengths,
    out_proj,
    residual,
    norm_gain,
    expert_ids,
    expert_slots,
    gate_probs,
    w_gate,
    w_up,
    w_down,
):
    attn = attention(queries, key_cache, value_cache, new_keys, new_values, lengths)
    R, K = lax.axis_size("req"), lax.axis_size("kv")
    M = 2 * K
    experts = R * M
    block, top = expert_ids.shape
    width = out_proj.shape[1]
    depth = out_proj.shape[0]
    hidden_units = w_gate.shape[2]
    capacity = top * block // experts + 1
    full, left = layout(R, capacity)
    parts = 16 // left if left else 1
    nch = CHUNKS
    cw = width // nch
    total_width = cw + (cw // parts if left else 0)
    r = lax.axis_index("req")

    codes = (r * (experts * capacity) + expert_ids * capacity + expert_slots).astype(F32)
    lanes = -(-R * block // 128) * 128
    by_lane = lax.dynamic_update_slice(
        jnp.full((top, lanes), -1.0, F32), codes.T, (jnp.int32(0), r * block)
    )
    by_row = jnp.pad(
        jnp.concatenate([codes, gate_probs], axis=1), ((0, 0), (0, lanes - 2 * top))
    )
    table = jnp.concatenate([by_lane, by_row], axis=0)

    member = np.arange(M)
    base = ((member // K) * R * K + member % K) * capacity
    slot = np.arange(full)
    code_of = (slot // capacity) * (experts * capacity) + slot % capacity
    targets = base[:, None] + np.where(slot < R * capacity, code_of, -(10**6))[None, :]
    targets = targets.reshape(-1).astype(np.float32)
    left_targets = np.full((parts, M, 16), -(10.0**6), np.float32)
    unpack = np.zeros((parts, M * max(left, 1), M * 16), np.float32)
    for q in range(parts if left else 0):
        for n in range(left):
            sigma = full + n
            code = (sigma // capacity) * (experts * capacity) + sigma % capacity
            left_targets[q, :, q * left + n] = base + code
            unpack[q, member * left + n, member * 16 + q * left + n] = 1.0
    shift = (r * (K * capacity)).astype(F32)
    targets = jnp.asarray(targets) + shift
    left_targets = jnp.asarray(left_targets.reshape(parts, M * 16)) + shift

    rows = M * (full + left)
    dims = {"R": R, "K": K, "full": full, "left": left, "top": top}
    vmem = pl.BlockSpec(memory_space=pltpu.VMEM)
    hbm = pl.BlockSpec(memory_space=pl.ANY)
    dma = pltpu.SemaphoreType.DMA
    outs = jax.ShapeDtypeStruct((block, width), BF16)
    return pl.pallas_call(
        functools.partial(layer_kernel, dims),
        out_shape=(outs, outs),
        in_specs=[vmem, hbm] + [vmem] * 9 + [hbm] * 3,
        out_specs=(vmem, vmem),
        scratch_shapes=[
            pltpu.VMEM((nch, depth, cw), BF16),
            pltpu.VMEM((nch, cw, hidden_units), BF16),
            pltpu.VMEM((nch, cw, hidden_units), BF16),
            pltpu.VMEM((nch, hidden_units, cw), BF16),
            pltpu.VMEM((nch, K * block, cw), BF16),
            pltpu.VMEM((nch, K * block, cw), BF16),
            pltpu.VMEM((nch, K, block, cw), BF16),
            pltpu.VMEM((nch, K - 1, block, cw), BF16),
            pltpu.VMEM((R, top + block, lanes), F32),
            pltpu.VMEM((M * full, R * block), BF16),
            pltpu.VMEM((parts, M * 16, R * block), BF16),
            pltpu.VMEM((R * block, M * full), BF16),
            pltpu.VMEM((parts, R * block, M * 16), BF16),
            pltpu.VMEM((nch, R, block, cw), BF16),
            pltpu.VMEM((nch, M, full, total_width), BF16),
            pltpu.VMEM((nch, M, full, total_width), BF16),
            pltpu.VMEM((rows, cw), BF16),
            pltpu.VMEM((rows, hidden_units), F32),
            pltpu.VMEM((rows, hidden_units), F32),
            pltpu.VMEM((nch, M, full, total_width), BF16),
            pltpu.VMEM((nch, M, full, total_width), BF16),
            pltpu.VMEM((nch, R, block, cw), BF16),
            pltpu.VMEM((nch, R - 1, block, cw), BF16),
            dma((4, nch)),
            dma((2, nch)),
            dma((2, nch, K - 1)),
            dma((2, R - 1)),
            dma((2, nch, R - 1)),
            dma((2, nch, M - 1)),
            dma((2, nch, M - 1)),
            dma((2, nch, R - 1)),
        ],
        compiler_params=pltpu.CompilerParams(
            collective_id=0, has_side_effects=True, vmem_limit_bytes=58 * 2**20
        ),
    )(
        attn.reshape(2, K * block, depth),
        out_proj,
        residual,
        norm_gain.reshape(1, width),
        table,
        targets.reshape(-1, 1),
        left_targets.reshape(parts, M * 16, 1),
        targets.reshape(1, -1),
        left_targets.reshape(parts, 1, M * 16),
        jnp.asarray(unpack, BF16),
        jnp.asarray(unpack.transpose(0, 2, 1), BF16),
        w_gate,
        w_up,
        w_down,
    )


def solution(mesh):
    return jax.shard_map(
        on_device,
        mesh=mesh,
        in_specs=(
            P("req", ("kv", "sec")),
            P("req", "kv", None, None),
            P("req", "kv", None, None),
            P("req", "kv", None),
            P("req", "kv", None),
            P("req"),
            P(("kv", "sec"), None),
            P(("req", "sec", "kv"), None),
            P(),
            P(("req", "sec", "kv"), None),
            P(("req", "sec", "kv"), None),
            P(("req", "sec", "kv"), None),
            P(("sec", "req", "kv"), None, None),
            P(("sec", "req", "kv"), None, None),
            P(("sec", "req", "kv"), None, None),
        ),
        out_specs=(P(("req", "sec", "kv"), None), P(("req", "sec", "kv"), None)),
        check_vma=False,
    )
```

time: 201 us -> 78 us (0.39)
  waiting for transfers between devices: 89.2 us -> 0 us
  Pallas kernels: 0 us -> 62.1 us
  blocking collectives: 55 us -> 0 us
  matrix products: 20 us -> 3.49 us
  between operations: 14.3 us -> 0.77 us
  local copies, waits for them, and re-layouts: 14.2 us -> 7.46 us
  starting transfers between devices: 3.65 us -> 0 us
    pallas_call x0 -> x1, Pallas kernels: none -> 62.1 us  [on_device(): pl.pallas_call(functools.partial(layer_kernel, dims), out_shape=(outs, ou...]
    all_to_all x1 -> x0, blocking collectives: 55 us -> none  [on_device(): lax.all_to_all(outgoing.reshape(expert_count, capacity, width), ('sec', '...]
    all_to_all x1 -> x0, waiting for transfers between devices: 50.5 us -> none  [on_device(): lax.all_to_all(finished.reshape(arrived.shape), ('sec', 'req', 'kv'), spl...]
    reduce_scatter x1 -> x0, waiting for transfers between devices: 38.7 us -> none  [on_device(): lax.psum_scatter(jnp.dot(attn, out_proj, preferred_element_type=jnp.float...]
    dot_general x6 -> x3, matrix products: 20 us -> 3.49 us  [the longest x1 1.96 us: attention(): jnp.einsum('thd,tpd->thp', query_heads, key_cache[:, 0], preferred_elemen...]
    reshape x6 -> x3, local copies, waits for them, and re-layouts: 9.1 us -> 2.61 us  [the longest x1 1.02 us: attention(): query_heads = queries.reshape(row_count, heads_here, head_size)]
    all_to_all x1 -> x0, starting transfers between devices: 3.61 us -> none  [on_device(): lax.all_to_all(finished.reshape(arrived.shape), ('sec', 'req', 'kv'), spl...]
    unnamed x17, local copies, waits for them, and re-layouts: 0.12 us -> 3.39 us
  transfers between devices with their start and end apart: 2 -> 0, of which waited for: 2 -> 0; matrix products, arithmetic and copies ran while one was open for 0% -> 0% of each run, Pallas kernels for 0% -> 0%
where the time goes in v1:
time: 78 us; the launch traced here: 77.6 us
  Pallas kernels  62.1 us (80%)
  local copies, waits for them, and re-layouts  7.46 us (10%)
  other arithmetic  3.73 us (5%)
  matrix products  3.49 us (4%)
    pallas_call x1, Pallas kernels, on_device(): pl.pallas_call(functools.partial(layer_kernel, dims), out_shape=(outs, ou...  62.1 us
    unnamed x17, local copies, waits for them, and re-layouts  3.39 us
    dot_general x1, matrix products, attention(): jnp.einsum('thd,tpd->thp', query_heads, key_cache[:, 0], preferred_elemen...  1.96 us

profile of v1, /device:TPU:0, one launch (start us, length us, event | category | flops | bytes accessed | tf_op | source)
XLA Modules:
  0.0 77.6 jit_solution(18124902406753393289)
XLA Ops:
  0.7 1.0 %reshape.42 = bf16[128,4,128]{2,1,0:T(4,128)(2,1)S(1)} reshape(bf16[128,512]{1,0:T(8,128)(2,1)} %param.19) | data formatting | bytes 262144 | tf_op jit(solution)/shard_map/reshape | solution.py:325
  1.7 0.7 iota_compare_fusion
  2.5 2.0 %fusion.13 = (f32[128,4]{1,0:T(8,128)S(1)}, f32[128,4,32]{2,1,0:T(4,128)S(1)}) fusion(bf16[128,4,128]{2,1,0:T(4,128)(2,1)S(1)} %reshape.42, bf16[128,1,32,128]{3,2,1,0:T(8,128)(2,1)} %param.20, pred[128,32]{1,0:T(8,128)(4,1)S(1)} %iota_compare_fusion), kind=kOutput, calls=%fused_computation.29 | convolution fusion | flops 4242944 | bytes 1251328 | tf_op jit(solution)/shard_map/thd,tpd->thp/dot_general | solution.py:327
  4.5 1.1 %fusion.7 = f32[128,1,4]{2,1,0:T(1,128)S(1)} fusion(bf16[128,4,128]{2,1,0:T(4,128)(2,1)S(1)} %reshape.42, bf16[128,128,1]{1,0,2:T(8,128)(2,1)} %bitcast.43), kind=kOutput, calls=%fused_computation.12 | convolution fusion | flops 131072 | bytes 165888 | tf_op jit(solution)/shard_map/thd,td->th/dot_general | solution.py:331
  5.6 0.1 copy.38
  5.7 0.4 fusion.4
  6.2 0.1 copy.40
  6.4 0.1 copy.41
  6.5 0.8 bitcast_convert_fusion
  7.2 0.5 fusion.1
  7.7 0.7 reshape_reshape.3.attn_ref
  8.5 0.1 copy.44
  8.6 0.1 copy.45
  8.7 0.1 dynamic_update_slice.3
  8.8 0.1 copy.46
  8.9 0.1 select_maximum_fusion
  9.0 0.6 pad_maximum_fusion.table_ref
  9.6 0.6 broadcast_add_fusion
  10.2 0.9 %copy.48.col_left_ref = f32[4,128,1]{2,1,0:T(8,128)} copy(f32[4,128,1]{1,0,2:T(4,128)S(1)} %get-tuple-element.5) | data formatting | bytes 4096 | tf_op jit(solution)/shard_map/reshape | solution.py:462
  11.0 0.5 add_bitcast_fusion
  11.6 0.7 copy.47.col_ref
  12.3 62.1 %shard_map.194 = (bf16[16,4096]{1,0:T(8,128)(2,1)}, bf16[16,4096]{1,0:T(8,128)(2,1)}) custom-call(bf16[2,64,512]{2,1,0:T(8,128)(2,1)} %reshape_reshape.3.attn_ref, bf16[512,4096]{1,0:T(8,128)(2,1)} %out_proj_hbm.1, bf16[16,4096]{1,0:T(8,128)(2,1)} %residual_ref.1, f32[1,4096]{1,0:T(1,128)} %bitcast.41, f32[24,128]{1,0:T(8,128)} %pad_maximum_fusion.table_ref, ...), custom_call_target="tpu_custom_call" | custom-call | tf_op jit(solution)/shard_map/pallas_call | solution.py:414
  74.4 1.6 %copy.56 = bf16[16,4096]{1,0:T(8,128)(2,1)} copy(bf16[16,4096]{1,0:T(8,128)(2,1)} %get-tuple-element.12) | data formatting | bytes 262144
  76.0 1.6 %copy.57 = bf16[16,4096]{1,0:T(8,128)(2,1)} copy(bf16[16,4096]{1,0:T(8,128)(2,1)} %get-tuple-element.13) | data formatting | bytes 262144
  (20 shorter events, 0.3 us)
Async XLA Ops:
  0.6 6.6 %copy-start = (bf16[128,1,32,128]{3,2,1,0:T(8,128)(2,1)S(1)}, bf16[128,1,32,128]{3,2,1,0:T(8,128)(2,1)}, u32[]{:S(2)}) copy-start(bf16[128,1,32,128]{3,2,1,0:T(8,128)(2,1)} %param.21) | copy-start | bytes 3145732
  0.6 8.9 %copy-start.4 = (f32[4,128]{1,0:T(4,128)S(1)}, f32[4,128]{1,0:T(4,128)}, u32[]{:S(2)}) copy-start(f32[4,128]{1,0:T(4,128)} %constant.36.clone) | copy-start | bytes 6148
  0.7 10.4 %copy-start.5 = (f32[128]{0:T(128)S(1)}, f32[128]{0:T(128)}, u32[]{:S(2)}) copy-start(f32[128]{0:T(128)} %constant.35.clone) | copy-start | bytes 1540
  0.7 7.8 %copy-start.1 = (s32[16,8]{0,1:T(8,128)S(1)}, s32[16,8]{0,1:T(8,128)}, u32[]{:S(2)}) copy-start(s32[16,8]{0,1:T(8,128)} %param.28) | copy-start | bytes 1540
  0.7 7.8 %copy-start.2 = (s32[16,8]{0,1:T(8,128)S(1)}, s32[16,8]{0,1:T(8,128)}, u32[]{:S(2)}) copy-start(s32[16,8]{0,1:T(8,128)} %param.29) | copy-start | bytes 1540
  0.7 8.1 %copy-start.3 = (f32[16,8]{0,1:T(8,128)S(1)}, f32[16,8]{0,1:T(8,128)}, u32[]{:S(2)}) copy-start(f32[16,8]{0,1:T(8,128)} %param.30) | copy-start | bytes 1540

commit v2 on v1

--- a/solution.py
+++ b/solution.py
@@ -28,15 +28,19 @@
 
 def layer_kernel(
     dims,
-    attn_ref,
+    query_ref,
+    key_hbm,
+    value_hbm,
+    new_key_ref,
+    new_value_ref,
+    length_ref,
     out_proj_hbm,
     residual_ref,
     gain_ref,
-    table_ref,
-    col_ref,
-    col_left_ref,
-    row_ref,
-    row_left_ref,
+    id_ref,
+    slot_ref,
+    prob_ref,
+    target_ref,
     unpack_ref,
     pack_ref,
     gate_hbm,
@@ -44,6 +48,9 @@
     down_hbm,
     stream_ref,
     moe_ref,
+    keys,
+    values,
+    attn,
     out_proj,
     w_gate,
     w_up,
@@ -52,11 +59,10 @@
     sib_in,
     part_out,
     part_in,
+    table,
     tables,
     pick,
-    pick_left,
     spread,
-    spread_left,
     tokens,
     disp_out,
     disp_in,
@@ -67,6 +73,7 @@
     ret_in,
     sum_out,
     sum_in,
+    cache_sem,
     weight_sem,
     sib_sem,
     part_sem,
@@ -101,9 +108,12 @@
         ][which]
         return pltpu.make_async_copy(src, dst.at[j], weight_sem.at[which, j])
 
-    for which in range(4):
-        for j in range(nch):
-            weight_copy(which, j).start()
+    key_copy = pltpu.make_async_copy(key_hbm.at[:, 0], keys, cache_sem.at[0])
+    value_copy = pltpu.make_async_copy(value_hbm.at[:, 0], values, cache_sem.at[1])
+    key_copy.start()
+    value_copy.start()
+    for j in range(nch):
+        weight_copy(0, j).start()
 
     def line(i):
         return lax.rem(r + i, R)
@@ -129,13 +139,11 @@
         )
     for i in range(1, R):
         pl.semaphore_signal(barrier, inc=1, device_id=(s, line(i), k), device_id_type=MESH)
-    pl.semaphore_wait(barrier, M + R - 2)
-
     def table_copy(i, me):
-        return remote(table_ref, tables.at[me], table_sem, (i - 1,), (s, line(i), k))
+        return remote(table, tables.at[me], table_sem, (i - 1,), (s, line(i), k))
 
     def sib_copy(j):
-        return remote(sib_out.at[j], sib_in.at[j], sib_sem, (j,), (1 - s, r, k))
+        return remote(sib_out.at[j, 1 - s], sib_in.at[j], sib_sem, (j,), (1 - s, r, k))
 
     def part_copy(j, i):
         to = lax.rem(k + i, K)
@@ -160,53 +168,118 @@
     def plane_before(i):
         return lax.rem(m - i + M, M)
 
+    code_scale = 1.0 * dims["capacity"]
+    first_code = (r * (R * M * dims["capacity"])).astype(F32)
+    codes_t = id_ref[...].astype(F32) * code_scale + slot_ref[...].astype(F32) + first_code
+    probs_t = prob_ref[...]
+    on_diagonal = lax.broadcasted_iota(jnp.int32, (16, 16), 0) == lax.broadcasted_iota(
+        jnp.int32, (16, 16), 1
+    )
+    lane = lax.broadcasted_iota(jnp.int32, (16, 128), 1)
+    filled = jnp.zeros((16, 128), F32)
+    for n in range(top):
+        for at, source in ((n, codes_t), (top + n, probs_t)):
+            column = jnp.sum(
+                jnp.where(on_diagonal, source[n : n + 1, :], 0.0), axis=1, keepdims=True
+            )
+            filled = jnp.where(lane == at, column, filled)
+    table[...] = filled
+
+    tokens_here = query_ref.shape[0]
+    head = keys.shape[2]
+    positions = keys.shape[1]
+    heads = query_ref.shape[1] // head
+    score_scale = 1.0 / head**0.5
+    square = (tokens_here, tokens_here)
+    length_column = jnp.sum(
+        jnp.where(
+            lax.broadcasted_iota(jnp.int32, square, 0) == lax.broadcasted_iota(jnp.int32, square, 1),
+            length_ref[...].astype(F32),
+            0.0,
+        ),
+        axis=1,
+        keepdims=True,
+    )
+    query_rows = 16 * heads
+    row_token = lax.broadcasted_iota(jnp.int32, (query_rows, 1), 0) % 16
+    key_lane = lax.broadcasted_iota(jnp.int32, (1, 16 * positions), 1)
+    same_token = key_lane // positions == row_token
+    position = (key_lane % positions).astype(F32)
+    own_token = lax.broadcasted_iota(jnp.int32, (1, 16), 1) == row_token
+    key_copy.wait()
+    value_copy.wait()
+    for which in range(1, 4):
+        for j in range(nch):
+            weight_copy(which, j).start()
+
+    def contract_last(a, b):
+        return lax.dot_general(a, b, (((1,), (1,)), ((), ())), preferred_element_type=F32)
+
+    for g in range(tokens_here // 16):
+        at = slice(g * 16, (g + 1) * 16)
+        query = jnp.concatenate(
+            [query_ref[at, h * head : (h + 1) * head] for h in range(heads)], axis=0
+        )
+        limit = jnp.concatenate([length_column[at]] * heads, axis=0)
+        score = contract_last(query, keys[at].reshape(16 * positions, head)) * score_scale
+        own = contract_last(query, new_key_ref[at, :]) * score_scale
+        score = jnp.where(same_token & (position < limit), score, -jnp.inf)
+        own = jnp.where(own_token, own, -jnp.inf)
+        highest = jnp.maximum(
+            jnp.max(score, axis=1, keepdims=True), jnp.max(own, axis=1, keepdims=True)
+        )
+        score = jnp.exp(score - highest)
+        own = jnp.exp(own - highest)
+        total = jnp.sum(score, axis=1, keepdims=True) + jnp.sum(own, axis=1, keepdims=True)
+        score = (score / total).astype(BF16)
+        own = (own / total).astype(BF16)
+        mixed = dot(score, values[at].reshape(16 * positions, head)) + dot(
+            own, new_value_ref[at, :]
+        )
+        mixed = mixed.astype(BF16)
+        for h in range(heads):
+            attn[at, h * head : (h + 1) * head] = mixed[h * 16 : (h + 1) * 16]
+
+    pl.semaphore_wait(barrier, M + R - 2)
     for i in range(1, R):
         table_copy(i, r).start()
-    tables[r] = table_ref[...]
+    tables[r] = filled
 
     @pl.loop(0, nch)
     def _(j):
         weight_copy(0, j).wait()
-        sib_out[j] = dot(attn_ref[1 - s], out_proj[j]).astype(BF16)
+        sib_out[j] = dot(attn[...], out_proj[j]).astype(BF16).reshape(2, K * 16, cw)
         sib_copy(j).start()
 
     @pl.loop(0, nch)
     def _(j):
-        own = dot(attn_ref[s], out_proj[j])
         sib_copy(j).wait_recv()
-        part_out[j] = (own + sib_in[j].astype(F32)).astype(BF16).reshape(K, 16, cw)
+        part_out[j] = (sib_out[j, s].astype(F32) + sib_in[j].astype(F32)).astype(BF16).reshape(K, 16, cw)
         for i in range(1, K):
             part_copy(j, i).start()
 
     for i in range(1, R):
         table_copy(i, before(i)).wait_recv()
-    codes = tables[0, 0:top, :]
-    for q in range(1, R):
-        codes = jnp.maximum(codes, tables[q, 0:top, :])
-    codes = codes[:, : R * 16]
-
-    def one_hot(targets):
-        total = jnp.zeros((targets.shape[0], R * 16), F32)
+    shift = (r * (K * dims["capacity"])).astype(F32)
+
+    def routes(q, targets):
+        chosen = jnp.zeros((16, targets.shape[1]), F32)
+        weights = jnp.zeros((16, targets.shape[1]), F32)
+        entry = tables[q]
         for n in range(top):
-            total = total + jnp.where(codes[n : n + 1, :] == targets, 1.0, 0.0)
-        return total.astype(BF16)
-
-    def weighted(q, targets):
-        total = jnp.zeros((16, targets.shape[1]), F32)
-        entry = tables[q, top : top + 16, :]
-        for n in range(top):
-            total = total + jnp.where(
-                entry[:, n : n + 1] == targets, entry[:, top + n : top + n + 1], 0.0
-            )
-        return total.astype(BF16)
-
-    pick[...] = one_hot(col_ref[...])
-    for q in range(parts):
-        pick_left[q] = one_hot(col_left_ref[q])
-    for q in range(R):
-        spread[q * 16 : (q + 1) * 16, :] = weighted(q, row_ref[...])
-        for n in range(parts):
-            spread_left[n, q * 16 : (q + 1) * 16, :] = weighted(q, row_left_ref[n])
+            hit = entry[:, n : n + 1] == targets
+            chosen = jnp.where(hit, 1.0, chosen)
+            weights = jnp.where(hit, entry[:, top + n : top + n + 1], weights)
+        return chosen, weights
+
+    for n in range(1 + parts):
+        targets = target_ref[n : n + 1, :] + shift
+        chosen = []
+        for q in range(R):
+            hits, weights = routes(q, targets)
+            chosen.append(hits)
+            spread[n, q * 16 : (q + 1) * 16, :] = weights.astype(BF16)
+        pick[n] = jnp.concatenate(chosen, axis=0).T.astype(BF16)
 
     def add_parts(j, squares):
         total = part_out[j, k].astype(F32)
@@ -233,11 +306,11 @@
         for i in range(1, R):
             token_copy(j, i, before(i)).wait_recv()
         held = tokens[j].reshape(R * 16, cw)
-        disp_out[j, :, :, 0:cw] = dot(pick[...], held).astype(BF16).reshape(M, full, cw)
+        disp_out[j, :, :, 0:cw] = dot(pick[0], held).astype(BF16).reshape(M, full, cw)
         if left:
-            extra = dot(pick_left[0], held[:, 0:lw])
+            extra = dot(pick[1], held[:, 0:lw])
             for q in range(1, parts):
-                extra = extra + dot(pick_left[q], held[:, q * lw : (q + 1) * lw])
+                extra = extra + dot(pick[1 + q], held[:, q * lw : (q + 1) * lw])
             disp_out[j, :, :, cw : cw + lw] = extra.astype(BF16).reshape(M, 16, lw)
         for i in range(1, M):
             plane_copy(disp_out, disp_in, disp_sem, j, i, m).start()
@@ -282,11 +355,11 @@
     def _(j):
         for i in range(1, M):
             plane_copy(ret_out, ret_in, ret_sem, j, i, plane_before(i)).wait_recv()
-        total = dot(spread[...], ret_in[j, :, :, 0:cw].reshape(M * full, cw))
+        total = dot(spread[0], ret_in[j, :, :, 0:cw].reshape(M * full, cw))
         if left:
             extra = ret_in[j, :, :, cw : cw + lw].reshape(M * 16, lw)
             total = total + jnp.concatenate(
-                [dot(spread_left[q], extra) for q in range(parts)], axis=1
+                [dot(spread[1 + q], extra) for q in range(parts)], axis=1
             )
         sum_out[j] = total.astype(BF16).reshape(R, 16, cw)
         for i in range(1, R):
@@ -316,32 +389,15 @@
             plane_copy(ret_out, ret_in, ret_sem, j, i, m).wait_send()
 
 
-def attention(queries, key_cache, value_cache, new_keys, new_values, lengths):
-    row_count, head_width = queries.shape
-    head_size = key_cache.shape[3]
-    positions = key_cache.shape[2]
-    heads_here = head_width // head_size
-    score_scale = 1.0 / head_size**0.5
-    query_heads = queries.reshape(row_count, heads_here, head_size)
-    score = (
-        jnp.einsum("thd,tpd->thp", query_heads, key_cache[:, 0], preferred_element_type=F32)
-        * score_scale
-    )
-    own_score = (
-        jnp.einsum("thd,td->th", query_heads, new_keys[:, 0], preferred_element_type=F32)
-        * score_scale
-    )
-    valid = jnp.arange(positions, dtype=jnp.int32)[None, :] < lengths[:, None]
-    score = jnp.where(valid[:, None, :], score, -jnp.inf)
-    highest = jnp.maximum(jnp.max(score, axis=-1), own_score)
-    raised = jnp.exp(score - highest[..., None])
-    own_raised = jnp.exp(own_score - highest)
-    denominator = jnp.sum(raised, axis=-1) + own_raised
-    weight = (raised / denominator[..., None]).astype(BF16)
-    own_weight = (own_raised / denominator).astype(BF16)
-    attn = jnp.einsum("thp,tpd->thd", weight, value_cache[:, 0], preferred_element_type=F32)
-    attn = attn + own_weight.astype(F32)[..., None] * new_values[:, 0].astype(F32)[:, None, :]
-    return attn.astype(BF16).reshape(row_count, head_width)
+def hand_over(stream_ref, moe_ref, stream_out, moe_out, sems):
+    copies = [
+        pltpu.make_async_copy(stream_ref, stream_out, sems.at[0]),
+        pltpu.make_async_copy(moe_ref, moe_out, sems.at[1]),
+    ]
+    for copy in copies:
+        copy.start()
+    for copy in copies:
+        copy.wait()
 
 
 def on_device(
@@ -361,7 +417,6 @@
     w_up,
     w_down,
 ):
-    attn = attention(queries, key_cache, value_cache, new_keys, new_values, lengths)
     R, K = lax.axis_size("req"), lax.axis_size("kv")
     M = 2 * K
     experts = R * M
@@ -375,17 +430,7 @@
     nch = CHUNKS
     cw = width // nch
     total_width = cw + (cw // parts if left else 0)
-    r = lax.axis_index("req")
-
-    codes = (r * (experts * capacity) + expert_ids * capacity + expert_slots).astype(F32)
-    lanes = -(-R * block // 128) * 128
-    by_lane = lax.dynamic_update_slice(
-        jnp.full((top, lanes), -1.0, F32), codes.T, (jnp.int32(0), r * block)
-    )
-    by_row = jnp.pad(
-        jnp.concatenate([codes, gate_probs], axis=1), ((0, 0), (0, lanes - 2 * top))
-    )
-    table = jnp.concatenate([by_lane, by_row], axis=0)
+    row_count, _, positions, head = key_cache.shape
 
     member = np.arange(M)
     base = ((member // K) * R * K + member % K) * capacity
@@ -401,35 +446,37 @@
             code = (sigma // capacity) * (experts * capacity) + sigma % capacity
             left_targets[q, :, q * left + n] = base + code
             unpack[q, member * left + n, member * 16 + q * left + n] = 1.0
-    shift = (r * (K * capacity)).astype(F32)
-    targets = jnp.asarray(targets) + shift
-    left_targets = jnp.asarray(left_targets.reshape(parts, M * 16)) + shift
+    targets = targets.reshape(1, -1)
+    if left:
+        targets = np.concatenate([targets, left_targets.reshape(parts, M * 16)], axis=0)
 
     rows = M * (full + left)
-    dims = {"R": R, "K": K, "full": full, "left": left, "top": top}
+    dims = {"R": R, "K": K, "full": full, "left": left, "top": top, "capacity": capacity}
     vmem = pl.BlockSpec(memory_space=pltpu.VMEM)
     hbm = pl.BlockSpec(memory_space=pl.ANY)
     dma = pltpu.SemaphoreType.DMA
     outs = jax.ShapeDtypeStruct((block, width), BF16)
-    return pl.pallas_call(
+    stream, moe_out = pl.pallas_call(
         functools.partial(layer_kernel, dims),
         out_shape=(outs, outs),
-        in_specs=[vmem, hbm] + [vmem] * 9 + [hbm] * 3,
+        in_specs=[vmem, hbm, hbm] + [vmem] * 3 + [hbm] + [vmem] * 8 + [hbm] * 3,
         out_specs=(vmem, vmem),
         scratch_shapes=[
+            pltpu.VMEM((row_count, positions, head), BF16),
+            pltpu.VMEM((row_count, positions, head), BF16),
+            pltpu.VMEM((row_count, depth), BF16),
             pltpu.VMEM((nch, depth, cw), BF16),
             pltpu.VMEM((nch, cw, hidden_units), BF16),
             pltpu.VMEM((nch, cw, hidden_units), BF16),
             pltpu.VMEM((nch, hidden_units, cw), BF16),
-            pltpu.VMEM((nch, K * block, cw), BF16),
+            pltpu.VMEM((nch, 2, K * block, cw), BF16),
             pltpu.VMEM((nch, K * block, cw), BF16),
             pltpu.VMEM((nch, K, block, cw), BF16),
             pltpu.VMEM((nch, K - 1, block, cw), BF16),
-            pltpu.VMEM((R, top + block, lanes), F32),
-            pltpu.VMEM((M * full, R * block), BF16),
-            pltpu.VMEM((parts, M * 16, R * block), BF16),
-            pltpu.VMEM((R * block, M * full), BF16),
-            pltpu.VMEM((parts, R * block, M * 16), BF16),
+            pltpu.VMEM((block, 128), F32),
+            pltpu.VMEM((R, block, 128), F32),
+            pltpu.VMEM((len(targets), M * full, R * block), BF16),
+            pltpu.VMEM((len(targets), R * block, M * full), BF16),
             pltpu.VMEM((nch, R, block, cw), BF16),
             pltpu.VMEM((nch, M, full, total_width), BF16),
             pltpu.VMEM((nch, M, full, total_width), BF16),
@@ -440,6 +487,7 @@
             pltpu.VMEM((nch, M, full, total_width), BF16),
             pltpu.VMEM((nch, R, block, cw), BF16),
             pltpu.VMEM((nch, R - 1, block, cw), BF16),
+            dma((2,)),
             dma((4, nch)),
             dma((2, nch)),
             dma((2, nch, K - 1)),
@@ -453,21 +501,32 @@
             collective_id=0, has_side_effects=True, vmem_limit_bytes=58 * 2**20
         ),
     )(
-        attn.reshape(2, K * block, depth),
+        queries,
+        key_cache,
+        value_cache,
+        new_keys[:, 0],
+        new_values[:, 0],
+        lengths.reshape(1, row_count),
         out_proj,
         residual,
         norm_gain.reshape(1, width),
-        table,
-        targets.reshape(-1, 1),
-        left_targets.reshape(parts, M * 16, 1),
-        targets.reshape(1, -1),
-        left_targets.reshape(parts, 1, M * 16),
+        expert_ids.T,
+        expert_slots.T,
+        gate_probs.T,
+        jnp.asarray(targets),
         jnp.asarray(unpack, BF16),
         jnp.asarray(unpack.transpose(0, 2, 1), BF16),
         w_gate,
         w_up,
         w_down,
     )
+    return pl.pallas_call(
+        hand_over,
+        out_shape=(outs, outs),
+        in_specs=[hbm, hbm],
+        out_specs=(hbm, hbm),
+        scratch_shapes=[dma((2,))],
+    )(stream, moe_out)
 
 
 def solution(mesh):

time: 78 us -> 75.8 us (0.972)
  Pallas kernels: 62.1 us -> 75 us
  local copies, waits for them, and re-layouts: 7.46 us -> 0 us
  other arithmetic: 3.73 us -> 0 us
  matrix products: 3.49 us -> 0 us
    pallas_call x0 -> x1, Pallas kernels: none -> 9.06 us  [on_device(): pl.pallas_call(hand_over, out_shape=(outs, outs), in_specs=[hbm, hbm], ou...]
    pallas_call x1, Pallas kernels: 62.1 us -> 65.9 us  [on_device(): pl.pallas_call(functools.partial(layer_kernel, dims), out_shape=(outs, ou...]
    dot_general x3 -> x0, matrix products: 3.49 us -> none  [the longest x1 1.96 us: attention(): jnp.einsum('thd,tpd->thp', query_heads, key_cache[:, 0], preferred_elemen...]
    unnamed x17 -> x0, local copies, waits for them, and re-layouts: 3.39 us -> none
    reshape x3 -> x0, local copies, waits for them, and re-layouts: 2.61 us -> none  [the longest x1 1.02 us: attention(): query_heads = queries.reshape(row_count, heads_here, head_size)]
where the time goes in v2:
time: 75.8 us; the launch traced here: 75.6 us
  Pallas kernels  75 us (99%)
    pallas_call x1, Pallas kernels, on_device(): pl.pallas_call(functools.partial(layer_kernel, dims), out_shape=(outs, ou...  65.9 us
    pallas_call x1, Pallas kernels, on_device(): pl.pallas_call(hand_over, out_shape=(outs, outs), in_specs=[hbm, hbm], ou...  9.06 us

profile of v2, /device:TPU:0, one launch (start us, length us, event | category | flops | bytes accessed | tf_op | source)
XLA Modules:
  0.0 75.6 jit_solution(14447840865633120216)
XLA Ops:
  0.6 65.9 %shard_map.185 = (bf16[16,4096]{1,0:T(8,128)(2,1)}, bf16[16,4096]{1,0:T(8,128)(2,1)}) custom-call(bf16[128,512]{1,0:T(8,128)(2,1)} %query_ref.1, bf16[128,1,32,128]{3,2,1,0:T(8,128)(2,1)} %key_hbm.1, bf16[128,1,32,128]{3,2,1,0:T(8,128)(2,1)} %value_hbm.1, bf16[128,128]{1,0:T(8,128)(2,1)} %bitcast.7, bf16[128,128]{1,0:T(8,128)(2,1)} %bitcast.8, ...), custom_call_target="tpu_custom_call" | custom-call | tf_op jit(solution)/shard_map/pallas_call | solution.py:459
  66.6 9.1 %shard_map.186 = (bf16[16,4096]{1,0:T(8,128)(2,1)}, bf16[16,4096]{1,0:T(8,128)(2,1)}) custom-call(bf16[16,4096]{1,0:T(8,128)(2,1)} %get-tuple-element.4.stream_ref, bf16[16,4096]{1,0:T(8,128)(2,1)} %get-tuple-element.5.moe_ref), custom_call_target="tpu_custom_call" | custom-call | tf_op jit(solution)/shard_map/pallas_call | solution.py:523

commit v3 on v2

--- a/solution.py
+++ b/solution.py
@@ -9,7 +9,7 @@
 from jax.sharding import PartitionSpec as P
 
 MESH = pl.DeviceIdType.MESH
-CHUNKS = 4
+CHUNKS = 8
 BF16 = jnp.bfloat16
 F32 = jnp.float32
 
@@ -389,15 +389,9 @@
             plane_copy(ret_out, ret_in, ret_sem, j, i, m).wait_send()
 
 
-def hand_over(stream_ref, moe_ref, stream_out, moe_out, sems):
-    copies = [
-        pltpu.make_async_copy(stream_ref, stream_out, sems.at[0]),
-        pltpu.make_async_copy(moe_ref, moe_out, sems.at[1]),
-    ]
-    for copy in copies:
-        copy.start()
-    for copy in copies:
-        copy.wait()
+def hand_over(stream_ref, moe_ref, stream_out, moe_out):
+    stream_out[...] = stream_ref[...]
+    moe_out[...] = moe_ref[...]
 
 
 def on_device(
@@ -523,9 +517,8 @@
     return pl.pallas_call(
         hand_over,
         out_shape=(outs, outs),
-        in_specs=[hbm, hbm],
-        out_specs=(hbm, hbm),
-        scratch_shapes=[dma((2,))],
+        in_specs=[vmem, vmem],
+        out_specs=(vmem, vmem),
     )(stream, moe_out)
 
 

time: 75.8 us -> 68.9 us (0.909)
  Pallas kernels: 75 us -> 68.1 us
    pallas_call x1, Pallas kernels: 9.06 us -> 1.68 us  [on_device(): pl.pallas_call(hand_over, out_shape=(outs, outs), in_specs=[vmem, vmem],...]
where the time goes in v3:
time: 68.9 us; the launch traced here: 68.8 us
  Pallas kernels  68.1 us (99%)
    pallas_call x1, Pallas kernels, on_device(): pl.pallas_call(functools.partial(layer_kernel, dims), out_shape=(outs, ou...  66.4 us
    pallas_call x1, Pallas kernels, on_device(): pl.pallas_call(hand_over, out_shape=(outs, outs), in_specs=[vmem, vmem],...  1.68 us

profile of v3, /device:TPU:0, one launch (start us, length us, event | category | flops | bytes accessed | tf_op | source)
XLA Modules:
  0.0 68.8 jit_solution(5440922541785696924)
XLA Ops:
  0.6 66.4 %shard_map.185 = (bf16[16,4096]{1,0:T(8,128)(2,1)}, bf16[16,4096]{1,0:T(8,128)(2,1)}) custom-call(bf16[128,512]{1,0:T(8,128)(2,1)} %query_ref.1, bf16[128,1,32,128]{3,2,1,0:T(8,128)(2,1)} %key_hbm.1, bf16[128,1,32,128]{3,2,1,0:T(8,128)(2,1)} %value_hbm.1, bf16[128,128]{1,0:T(8,128)(2,1)} %bitcast.7, bf16[128,128]{1,0:T(8,128)(2,1)} %bitcast.8, ...), custom_call_target="tpu_custom_call" | custom-call | tf_op jit(solution)/shard_map/pallas_call | solution.py:453
  67.1 1.7 %shard_map.186 = (bf16[16,4096]{1,0:T(8,128)(2,1)}, bf16[16,4096]{1,0:T(8,128)(2,1)}) custom-call(bf16[16,4096]{1,0:T(8,128)(2,1)} %get-tuple-element.4.stream_ref, bf16[16,4096]{1,0:T(8,128)(2,1)} %get-tuple-element.5.moe_ref), custom_call_target="tpu_custom_call" | custom-call | tf_op jit(solution)/shard_map/pallas_call | solution.py:517

commit v4 on v3

--- a/solution.py
+++ b/solution.py
@@ -73,6 +73,10 @@
     ret_in,
     sum_out,
     sum_in,
+    scales,
+    slot_scale_out,
+    slot_scale_in,
+    row_scale,
     cache_sem,
     weight_sem,
     sib_sem,
@@ -82,6 +86,8 @@
     disp_sem,
     ret_sem,
     sum_sem,
+    scale_sem,
+    slot_scale_sem,
 ):
     R, K, full, left = dims["R"], dims["K"], dims["full"], dims["left"]
     top = dims["top"]
@@ -161,6 +167,19 @@
     def sum_copy(j, i):
         to = line(i)
         return remote(sum_out.at[j, to], sum_in.at[j, i - 1], sum_sem, (j, i - 1), (s, to, k))
+
+    def scale_copy(i, me):
+        return remote(scales.at[me], scales.at[me], scale_sem, (i - 1,), (s, line(i), k))
+
+    def slot_scale_copy(i, me):
+        p = plane(i)
+        return remote(
+            slot_scale_out.at[p],
+            slot_scale_in.at[me],
+            slot_scale_sem,
+            (i - 1,),
+            (p // K, r, lax.rem(p, K)),
+        )
 
     def before(i):
         return lax.rem(r - i + R, R)
@@ -289,17 +308,16 @@
         value = (residual_ref[:, cols(j)].astype(F32) + total).astype(BF16)
         stream_ref[:, cols(j)] = value
         value = value.astype(F32)
+        tokens[j, r] = (value * gain_ref[:, cols(j)]).astype(BF16)
+        for i in range(1, R):
+            token_copy(j, i, r).start()
         return squares + jnp.sum(value * value, axis=1, keepdims=True)
 
     squares = lax.fori_loop(0, nch, add_parts, jnp.zeros((16, 1), F32))
     scale = lax.rsqrt(squares * (1.0 / width) + 1e-06)
-
-    @pl.loop(0, nch)
-    def _(j):
-        value = stream_ref[:, cols(j)].astype(F32)
-        tokens[j, r] = (value * scale * gain_ref[:, cols(j)]).astype(BF16)
-        for i in range(1, R):
-            token_copy(j, i, r).start()
+    scales[r] = jnp.broadcast_to(scale, (16, 128))
+    for i in range(1, R):
+        scale_copy(i, r).start()
 
     @pl.loop(0, nch)
     def _(j):
@@ -316,6 +334,36 @@
             plane_copy(disp_out, disp_in, disp_sem, j, i, m).start()
         disp_in[j, m] = disp_out[j, m]
 
+    for i in range(1, R):
+        scale_copy(i, before(i)).wait_recv()
+    scale = scales[...].reshape(R * 16, 128)
+    scale_high = scale.astype(BF16)
+    scale_low = (scale - scale_high.astype(F32)).astype(BF16)
+
+    def slot_scales(n):
+        picked = dot(pick[n], scale_high) + dot(pick[n], scale_low)
+        return picked.reshape(M, full, 128)
+
+    slot_scale_out[:, 0:full, :] = slot_scales(0)
+    slot_scale_out[:, full : full + 8, :] = (
+        slot_scales(1)[:, 0:8, :] if left else jnp.zeros((M, 8, 128), F32)
+    )
+    for i in range(1, M):
+        slot_scale_copy(i, m).start()
+    slot_scale_in[m] = slot_scale_out[m]
+
+    for i in range(1, R):
+        table_copy(i, r).wait_send()
+        scale_copy(i, r).wait_send()
+
+    @pl.loop(0, nch)
+    def _(j):
+        sib_copy(j).wait_send()
+        for i in range(1, K):
+            part_copy(j, i).wait_send()
+        for i in range(1, R):
+            token_copy(j, i, r).wait_send()
+
     gate_acc[...] = jnp.zeros_like(gate_acc)
     up_acc[...] = jnp.zeros_like(up_acc)
 
@@ -333,8 +381,17 @@
         gate_acc[...] += dot(rows_in[...], w_gate[j])
         up_acc[...] += dot(rows_in[...], w_up[j])
 
-    gate_out = gate_acc[...]
-    hidden = (gate_out / (1.0 + jnp.exp(-gate_out)) * up_acc[...]).astype(BF16)
+    for i in range(1, M):
+        slot_scale_copy(i, plane_before(i)).wait_recv()
+    row_scale[0 : M * full, :] = slot_scale_in[:, 0:full, :].reshape(M * full, 128)
+    if left:
+        for p in range(M):
+            at = M * full + p * left
+            row_scale[at : at + left, :] = slot_scale_in[p, full : full + left, :]
+    row_factor = row_scale[:, 0:1]
+    gate_out = gate_acc[...] * row_factor
+    up_out = up_acc[...] * row_factor
+    hidden = (gate_out / (1.0 + jnp.exp(-gate_out)) * up_out).astype(BF16)
 
     @pl.loop(0, nch)
     def _(j):
@@ -351,6 +408,14 @@
             plane_copy(ret_out, ret_in, ret_sem, j, i, m).start()
         ret_in[j, m] = ret_out[j, m]
 
+    for i in range(1, M):
+        slot_scale_copy(i, m).wait_send()
+
+    @pl.loop(0, nch)
+    def _(j):
+        for i in range(1, M):
+            plane_copy(disp_out, disp_in, disp_sem, j, i, m).wait_send()
+
     @pl.loop(0, nch)
     def _(j):
         for i in range(1, M):
@@ -367,26 +432,18 @@
 
     @pl.loop(0, nch)
     def _(j):
+        for i in range(1, M):
+            plane_copy(ret_out, ret_in, ret_sem, j, i, m).wait_send()
+
+    @pl.loop(0, nch)
+    def _(j):
         total = sum_out[j, r].astype(F32)
         for i in range(1, R):
             sum_copy(j, i).wait_recv()
             total = total + sum_in[j, i - 1].astype(F32)
         moe_ref[:, cols(j)] = total.astype(BF16)
-
-    for i in range(1, R):
-        table_copy(i, r).wait_send()
-
-    @pl.loop(0, nch)
-    def _(j):
-        sib_copy(j).wait_send()
-        for i in range(1, K):
-            part_copy(j, i).wait_send()
         for i in range(1, R):
-            token_copy(j, i, r).wait_send()
             sum_copy(j, i).wait_send()
-        for i in range(1, M):
-            plane_copy(disp_out, disp_in, disp_sem, j, i, m).wait_send()
-            plane_copy(ret_out, ret_in, ret_sem, j, i, m).wait_send()
 
 
 def hand_over(stream_ref, moe_ref, stream_out, moe_out):
@@ -481,6 +538,10 @@
             pltpu.VMEM((nch, M, full, total_width), BF16),
             pltpu.VMEM((nch, R, block, cw), BF16),
             pltpu.VMEM((nch, R - 1, block, cw), BF16),
+            pltpu.VMEM((R, block, 128), F32),
+            pltpu.VMEM((M, full + 8, 128), F32),
+            pltpu.VMEM((M, full + 8, 128), F32),
+            pltpu.VMEM((rows, 128), F32),
             dma((2,)),
             dma((4, nch)),
             dma((2, nch)),
@@ -490,6 +551,8 @@
             dma((2, nch, M - 1)),
             dma((2, nch, M - 1)),
             dma((2, nch, R - 1)),
+            dma((2, R - 1)),
+            dma((2, M - 1)),
         ],
         compiler_params=pltpu.CompilerParams(
             collective_id=0, has_side_effects=True, vmem_limit_bytes=58 * 2**20

time: 68.9 us -> 65.1 us (0.945)
  Pallas kernels: 68.1 us -> 64.3 us
    pallas_call x1, Pallas kernels: 66.4 us -> 62.6 us  [on_device(): pl.pallas_call(functools.partial(layer_kernel, dims), out_shape=(outs, ou...]
where the time goes in v4:
time: 65.1 us; the launch traced here: 64.9 us
  Pallas kernels  64.3 us (99%)
    pallas_call x1, Pallas kernels, on_device(): pl.pallas_call(functools.partial(layer_kernel, dims), out_shape=(outs, ou...  62.6 us
    pallas_call x1, Pallas kernels, on_device(): pl.pallas_call(hand_over, out_shape=(outs, outs), in_specs=[vmem, vmem],...  1.68 us

profile of v4, /device:TPU:0, one launch (start us, length us, event | category | flops | bytes accessed | tf_op | source)
XLA Modules:
  0.0 64.9 jit_solution(4523163746856907231)
XLA Ops:
  0.6 62.6 %shard_map.185 = (bf16[16,4096]{1,0:T(8,128)(2,1)}, bf16[16,4096]{1,0:T(8,128)(2,1)}) custom-call(bf16[128,512]{1,0:T(8,128)(2,1)} %query_ref.1, bf16[128,1,32,128]{3,2,1,0:T(8,128)(2,1)} %key_hbm.1, bf16[128,1,32,128]{3,2,1,0:T(8,128)(2,1)} %value_hbm.1, bf16[128,128]{1,0:T(8,128)(2,1)} %bitcast.7, bf16[128,128]{1,0:T(8,128)(2,1)} %bitcast.8, ...), custom_call_target="tpu_custom_call" | custom-call | tf_op jit(solution)/shard_map/pallas_call | solution.py:510
  63.3 1.7 %shard_map.186 = (bf16[16,4096]{1,0:T(8,128)(2,1)}, bf16[16,4096]{1,0:T(8,128)(2,1)}) custom-call(bf16[16,4096]{1,0:T(8,128)(2,1)} %get-tuple-element.4.stream_ref, bf16[16,4096]{1,0:T(8,128)(2,1)} %get-tuple-element.5.moe_ref), custom_call_target="tpu_custom_call" | custom-call | tf_op jit(solution)/shard_map/pallas_call | solution.py:580

commit v5 on v4

--- a/solution.py
+++ b/solution.py
@@ -10,6 +10,7 @@
 
 MESH = pl.DeviceIdType.MESH
 CHUNKS = 8
+LAG = 2
 BF16 = jnp.bfloat16
 F32 = jnp.float32
 
@@ -77,6 +78,7 @@
     slot_scale_out,
     slot_scale_in,
     row_scale,
+    squares,
     cache_sem,
     weight_sem,
     sib_sem,
@@ -300,7 +302,7 @@
             spread[n, q * 16 : (q + 1) * 16, :] = weights.astype(BF16)
         pick[n] = jnp.concatenate(chosen, axis=0).T.astype(BF16)
 
-    def add_parts(j, squares):
+    def add_parts(j):
         total = part_out[j, k].astype(F32)
         for i in range(1, K):
             part_copy(j, i).wait_recv()
@@ -311,16 +313,9 @@
         tokens[j, r] = (value * gain_ref[:, cols(j)]).astype(BF16)
         for i in range(1, R):
             token_copy(j, i, r).start()
-        return squares + jnp.sum(value * value, axis=1, keepdims=True)
-
-    squares = lax.fori_loop(0, nch, add_parts, jnp.zeros((16, 1), F32))
-    scale = lax.rsqrt(squares * (1.0 / width) + 1e-06)
-    scales[r] = jnp.broadcast_to(scale, (16, 128))
-    for i in range(1, R):
-        scale_copy(i, r).start()
-
-    @pl.loop(0, nch)
-    def _(j):
+        squares[...] += jnp.sum(value * value, axis=1, keepdims=True)
+
+    def dispatch(j):
         for i in range(1, R):
             token_copy(j, i, before(i)).wait_recv()
         held = tokens[j].reshape(R * 16, cw)
@@ -333,6 +328,25 @@
         for i in range(1, M):
             plane_copy(disp_out, disp_in, disp_sem, j, i, m).start()
         disp_in[j, m] = disp_out[j, m]
+
+    squares[...] = jnp.zeros_like(squares)
+
+    @pl.loop(0, nch + LAG)
+    def _(j):
+        @pl.when(j < nch)
+        def _():
+            add_parts(j)
+
+        @pl.when(j == nch - 1)
+        def _():
+            scale = lax.rsqrt(squares[...] * (1.0 / width) + 1e-06)
+            scales[r] = jnp.broadcast_to(scale, (16, 128))
+            for i in range(1, R):
+                scale_copy(i, r).start()
+
+        @pl.when(j >= LAG)
+        def _():
+            dispatch(j - LAG)
 
     for i in range(1, R):
         scale_copy(i, before(i)).wait_recv()
@@ -542,6 +556,7 @@
             pltpu.VMEM((M, full + 8, 128), F32),
             pltpu.VMEM((M, full + 8, 128), F32),
             pltpu.VMEM((rows, 128), F32),
+            pltpu.VMEM((block, 1), F32),
             dma((2,)),
             dma((4, nch)),
             dma((2, nch)),

time: 65.1 us -> 63.2 us (0.971)
  Pallas kernels: 64.3 us -> 62.4 us
    pallas_call x1, Pallas kernels: 62.6 us -> 60.7 us  [on_device(): pl.pallas_call(functools.partial(layer_kernel, dims), out_shape=(outs, ou...]
where the time goes in v5:
time: 63.2 us; the launch traced here: 63 us
  Pallas kernels  62.4 us (99%)
  between operations  0.64 us (1%)
    pallas_call x1, Pallas kernels, on_device(): pl.pallas_call(functools.partial(layer_kernel, dims), out_shape=(outs, ou...  60.7 us
    pallas_call x1, Pallas kernels, on_device(): pl.pallas_call(hand_over, out_shape=(outs, outs), in_specs=[vmem, vmem],...  1.68 us

profile of v5, /device:TPU:0, one launch (start us, length us, event | category | flops | bytes accessed | tf_op | source)
XLA Modules:
  0.0 63.0 jit_solution(9805573941188849566)
XLA Ops:
  0.6 60.7 %shard_map.185 = (bf16[16,4096]{1,0:T(8,128)(2,1)}, bf16[16,4096]{1,0:T(8,128)(2,1)}) custom-call(bf16[128,512]{1,0:T(8,128)(2,1)} %query_ref.1, bf16[128,1,32,128]{3,2,1,0:T(8,128)(2,1)} %key_hbm.1, bf16[128,1,32,128]{3,2,1,0:T(8,128)(2,1)} %value_hbm.1, bf16[128,128]{1,0:T(8,128)(2,1)} %bitcast.7, bf16[128,128]{1,0:T(8,128)(2,1)} %bitcast.8, ...), custom_call_target="tpu_custom_call" | custom-call | tf_op jit(solution)/shard_map/pallas_call | solution.py:524
  61.4 1.7 %shard_map.186 = (bf16[16,4096]{1,0:T(8,128)(2,1)}, bf16[16,4096]{1,0:T(8,128)(2,1)}) custom-call(bf16[16,4096]{1,0:T(8,128)(2,1)} %get-tuple-element.4.stream_ref, bf16[16,4096]{1,0:T(8,128)(2,1)} %get-tuple-element.5.moe_ref), custom_call_target="tpu_custom_call" | custom-call | tf_op jit(solution)/shard_map/pallas_call | solution.py:595
